TPU v7x, 512 devices: a whole 4x8x8 slice. The times are simulated.
512 devices in a mesh: gx: 64 (over z_lo, x, y), gy: 8 (over z_hi, core).
Axes of the slice: x: 4, y: 8, z: 8 (z_hi: 4, z_lo: 2; z = z_hi * 2 + z_lo), core: 2. Of those that a mesh axis runs over, the one named last changes fastest.
Arguments:
- position: float32 [3, 2097152], P(None, ('gx', 'gy')), may hold values from 0.05 to 0.95, as said below
- momentum: float32 [3, 2097152], P(None, ('gx', 'gy')), may hold values from -1.6 to 1.6, as said below
- cell_first: int32 [3, 2097152], P(None, ('gx', 'gy')), may hold values from 0 to 255, as said below
- cell_second: int32 [3, 2097152], P(None, ('gx', 'gy')), may hold values from 0 to 255, as said below
- destination: int32 [2097152], P(('gx', 'gy')), may hold values from 0 to 4, as said below
- slot_index: int32 [2097152], P(('gx', 'gy')), may hold values from 0 to 4095, as said below
- pull_position: float32 [3, 2097152], P(None, ('gx', 'gy')), may hold values from -6 to 6
- pull_momentum: float32 [3, 2097152], P(None, ('gx', 'gy')), may hold values from -6 to 6
Outputs:
- grad_position: float32 [3, 2097152], P(None, ('gx', 'gy'))
- grad_momentum: float32 [3, 2097152], P(None, ('gx', 'gy'))
Inputs may be any that keep to these rules, and one draw needn't show every extreme that they name: `destination`: 0: the particle stays on its device; 1 and 2: it moves to the next and to the previous device along gx; 3 and 4: to the next and to the previous device along gy (both axes wrap). From the particles of one device at most 256 go to each of its four neighbours, and in every draw some device sends exactly 256 to one neighbour. Between two neighbouring devices as many particles move one way as the other. A particle that moves to the next (previous) device along an axis lies in the last (first) cell layer of its device along that axis in cell_first. Over all particles the destination device and slot_index fill every index of every device exactly once. `cell_first`: the first component is below 2, the second below 8, the third below 256. `cell_second`: the cell_first of the particle that lands at this index, moved with it: a particle moving along gx goes from the last layer to the first or from the first to the last, likewise along gy; other components stay. The first component is below 2, the second below 8, the third below 256. `position`: A particle's drift_one leaves its cell along an axis exactly where destination sends it across that axis, in that direction. `momentum`: momenta of particles that move carry them across the cell face toward their destination.
All inputs are finite; a program needn't handle non-finite values.
Results may differ from a plain program's by a relative error of at most 0.000058.
Values sent between devices are 32-bit elements; how exact they have to be, the bound alone decides.
No kernel may reach another device: no remote copies, remote signals or barrier semaphores. Data moves between devices by JAX's collectives and lax.ppermute only.
A program may use at most 64 MiB of HBM per device.

v0:
```python
import jax
import jax.numpy as jnp
from jax import lax
from jax.sharding import PartitionSpec as P

CX = 2
CY = 8
NZ = 256
MOVE_MOST = 256
highest = lax.Precision.HIGHEST
step_size = 0.25
strength = 0.02


def with_halo(x, sides, width):
    for axis, dim in sides:
        peers, length = (lax.axis_size(axis), x.shape[dim])
        up = [(i, (i + 1) % peers) for i in range(peers)]
        down = [(j, i) for i, j in up]
        last = lax.slice_in_dim(x, length - width, length, axis=dim)
        first = lax.slice_in_dim(x, 0, width, axis=dim)
        before = lax.ppermute(last, axis, up)
        after = lax.ppermute(first, axis, down)
        x = jnp.concatenate([before, x, after], axis=dim)
    return x


def kernel_block(targets, sources, extent, reach_cells):
    distance = jnp.abs(targets[:, None] - sources[None, :])
    distance = jnp.minimum(distance, extent - distance)
    return jnp.exp(-distance.astype(jnp.float32) / reach_cells)


def cloud_weights(cell_block, frac_block, plane_count, row_count, depth_cells):
    index_row = jnp.arange(row_count, dtype=jnp.int32)[:, None]
    corner = (cell_block[1] * plane_count + cell_block[0])[None, :]
    hit_base = (index_row == corner).astype(jnp.float32)
    hit_east = (index_row == corner + 1).astype(jnp.float32)
    hit_north = (index_row == corner + plane_count).astype(jnp.float32)
    hit_both = (index_row == corner + plane_count + 1).astype(jnp.float32)
    west_weight = (1.0 - frac_block[0])[None, :]
    east_weight = frac_block[0][None, :]
    south_weight = (1.0 - frac_block[1])[None, :]
    north_weight = frac_block[1][None, :]
    planar = (
        hit_base * (west_weight * south_weight)
        + hit_east * (east_weight * south_weight)
        + hit_north * (west_weight * north_weight)
        + hit_both * (east_weight * north_weight)
    )
    slope_east = (hit_east - hit_base) * south_weight + (hit_both - hit_north) * north_weight
    slope_north = (hit_north - hit_base) * west_weight + (hit_both - hit_east) * east_weight
    index_depth = jnp.arange(depth_cells, dtype=jnp.int32)[:, None]
    lower_hit = (index_depth == cell_block[2][None, :]).astype(jnp.float32)
    upper_hit = (index_depth == ((cell_block[2] + 1) % depth_cells)[None, :]).astype(jnp.float32)
    vertical = lower_hit * (1.0 - frac_block[2])[None, :] + upper_hit * frac_block[2][None, :]
    slope_up = upper_hit - lower_hit
    return (planar, slope_east, slope_north, vertical, slope_up)


def particle_blocks(values):
    particle_count = values.shape[1]
    block_width = min(512, particle_count)
    return values.reshape(values.shape[0], particle_count // block_width, block_width).transpose(
        1, 0, 2
    )


def deposit(scales, cell_ids, offsets):
    layers = scales.shape[0]
    row_count = (CY + 1) * (CX + 1)

    def add_block(running, pieces):
        cell_block, frac_block, scale_block = pieces
        weights = cloud_weights(cell_block, frac_block, CX + 1, row_count, NZ)
        spread = scale_block[:, None, :] * weights[0][None]
        return (running + jnp.einsum("crb,zb->crz", spread, weights[3], precision=highest), None)

    initial = jnp.zeros((layers, row_count, NZ), jnp.float32)
    running, unused = lax.scan(
        add_block,
        initial,
        (particle_blocks(cell_ids), particle_blocks(offsets), particle_blocks(scales)),
    )
    return running.reshape(layers, CY + 1, CX + 1, NZ)


def sample_fields(fields, cell_ids, offsets, slopes):
    layers = fields.shape[0]
    row_count = fields.shape[1] * fields.shape[2]
    flattened = fields.reshape(layers * row_count, NZ)

    def one_block(pieces):
        cell_block, frac_block = pieces
        block_width = cell_block.shape[1]
        weights = cloud_weights(cell_block, frac_block, fields.shape[2], row_count, NZ)
        columns = jnp.concatenate([weights[3], weights[4]], 1) if slopes else weights[3]
        contracted = jnp.dot(
            flattened, columns, precision=highest, preferred_element_type=jnp.float32
        )
        contracted = contracted.reshape(layers, row_count, -1)
        nearby = contracted[:, :, :block_width]
        results = [jnp.sum(nearby * weights[0][None], axis=1)]
        if slopes:
            results.append(jnp.sum(nearby * weights[1][None], axis=1))
            results.append(jnp.sum(nearby * weights[2][None], axis=1))
            results.append(jnp.sum(contracted[:, :, block_width:] * weights[0][None], axis=1))
        return jnp.stack(results, 0)

    blocked = lax.map(one_block, (particle_blocks(cell_ids), particle_blocks(offsets)))
    return blocked.transpose(1, 2, 0, 3).reshape(blocked.shape[1], layers, cell_ids.shape[1])


def fold_planes(slab):
    planes = slab.shape[2]
    widened = with_halo(slab, (("gx", 2),), 2)
    return jnp.concatenate(
        [
            widened[:, :, 0:1],
            widened[:, :, 1:2] + widened[:, :, 2:3],
            widened[:, :, 3 : planes + 1],
            widened[:, :, planes + 1 : planes + 2] + widened[:, :, planes + 2 : planes + 3],
            widened[:, :, planes + 3 : planes + 4],
        ],
        axis=2,
    )


def smooth_depth(field):
    depth_cells = field.shape[-1]
    axis_cells = jnp.arange(depth_cells, dtype=jnp.int32)
    matrix = kernel_block(axis_cells, axis_cells, depth_cells, depth_cells / 16.0)
    return jnp.dot(
        field.reshape(-1, depth_cells),
        matrix,
        precision=highest,
        preferred_element_type=jnp.float32,
    ).reshape(field.shape)


def sum_lines(field):
    members = lax.axis_size("gy")
    band_rows = field.shape[1]
    own_rows = band_rows - 1
    extent = own_rows * members
    reach_cells = extent / 4.0
    anchor = lax.axis_index("gy") * own_rows
    targets = (anchor + jnp.arange(-1, own_rows + 2, dtype=jnp.int32)) % extent
    initial = jnp.zeros((field.shape[0], own_rows + 3, field.shape[2], field.shape[3]), jnp.float32)
    gathered = lax.all_gather(field, "gy", axis=1, tiled=True)
    length = gathered.shape[1]
    positions = jnp.arange(length, dtype=jnp.int32)
    sources = (positions // band_rows * own_rows + positions % band_rows) % extent
    weights = kernel_block(targets, sources, extent, reach_cells)
    return initial + jnp.einsum("ab,cbxz->caxz", weights, gathered, precision=highest)


def force_field(density):
    potential = sum_lines(smooth_depth(fold_planes(density)))
    potential = strength * potential
    centre = potential[:, 1:-1, 1:-1]
    push_east = -0.5 * (potential[:, 1:-1, 2:] - potential[:, 1:-1, :-2])
    push_north = -0.5 * (potential[:, 2:, 1:-1] - potential[:, :-2, 1:-1])
    push_up = -0.5 * (jnp.roll(centre, -1, 3) - jnp.roll(centre, 1, 3))
    return jnp.concatenate([push_east, push_north, push_up], 0)


def force_pullback(pushes, cell_ids, offsets, pull_force):
    folded = fold_planes(deposit(pull_force, cell_ids, offsets))
    across = 0.5 * (folded[0:1, :, 2:] - folded[0:1, :, :-2])
    upward = folded[2:3, :, 1:-1]
    across = across + 0.5 * (jnp.roll(upward, -1, 3) - jnp.roll(upward, 1, 3))
    line_sums = sum_lines(jnp.concatenate([across, folded[1:2, :, 1:-1]], 0))
    summed = line_sums[0:1, 1:-1] + 0.5 * (line_sums[1:2, 2:] - line_sums[1:2, :-2])
    density_pull = strength * smooth_depth(summed)
    sampled = sample_fields(jnp.concatenate([pushes, density_pull], 0), cell_ids, offsets, True)
    slopes = sampled[1:]
    return jnp.sum(slopes[:, :3] * pull_force[None], axis=1) + slopes[:, 3]


def pack_moves(destination, capacity):
    particle_count = destination.shape[0]
    grouped = jnp.argsort(destination, stable=True)
    group_size = jnp.sum(
        (destination[None, :] == jnp.arange(5, dtype=jnp.int32)[:, None]).astype(jnp.int32), axis=1
    )
    earlier = jnp.arange(5, dtype=jnp.int32)[None, :] < jnp.arange(5, dtype=jnp.int32)[:, None]
    opening = jnp.sum(jnp.where(earlier, group_size[None, :], 0), axis=1)
    lane_index = jnp.arange(capacity, dtype=jnp.int32)
    chosen = jnp.stack(
        [
            grouped[jnp.minimum(opening[move_code] + lane_index, particle_count - 1)]
            for move_code in range(1, 5)
        ],
        0,
    )
    filled = lane_index[None, :] < group_size[1:5, None]
    return (chosen, filled)


def trade_pairs(outward_x, outward_y):
    widened_x = with_halo(outward_x, (("gx", 1),), 1)
    widened_y = with_halo(outward_y, (("gy", 1),), 1)
    return (widened_x[:, 0], widened_x[:, 3], widened_y[:, 0], widened_y[:, 3])


def local(
    position,
    momentum,
    cell_first,
    cell_second,
    destination,
    slot_index,
    pull_position,
    pull_momentum,
):
    particle_count = position.shape[1]
    unit_mass = jnp.ones((1, particle_count), jnp.float32)
    drift_one = position + step_size * momentum
    push_one = force_field(deposit(unit_mass, cell_first, drift_one))
    kick_one = momentum + step_size * sample_fields(push_one, cell_first, drift_one, False)[0]
    eastward = (destination == 1).astype(jnp.float32) - (destination == 2).astype(jnp.float32)
    northward = (destination == 3).astype(jnp.float32) - (destination == 4).astype(jnp.float32)
    shift_cells = jnp.stack([eastward, northward, jnp.zeros_like(eastward)], 0)
    payload = jnp.concatenate([drift_one - shift_cells, kick_one], 0)
    chosen, filled = pack_moves(destination, MOVE_MOST)
    slot_marks = jnp.where(filled, slot_index[chosen], particle_count).astype(jnp.float32)
    parcel = jnp.where(filled[None], payload[:, chosen], 0.0)
    parcel = jnp.concatenate([parcel, slot_marks[None]], 0)
    arrivals = trade_pairs(
        jnp.stack([parcel[:, 1], parcel[:, 0]], 1), jnp.stack([parcel[:, 3], parcel[:, 2]], 1)
    )
    arrivals = jnp.concatenate(arrivals, 1)
    received = arrivals[6].astype(jnp.int32)
    staying = jnp.where(destination == 0, slot_index, particle_count)
    placed = jnp.concatenate([staying, received], 0)
    arrived = (
        jnp.zeros((6, particle_count), jnp.float32)
        .at[:, placed]
        .set(jnp.concatenate([payload, arrivals[:6]], 1), mode="drop")
    )
    drift_two = arrived[:3] + step_size * arrived[3:]
    push_two = force_field(deposit(unit_mass, cell_second, drift_two))
    grad_drift_two = pull_position + force_pullback(
        push_two, cell_second, drift_two, step_size * pull_momentum
    )
    grad_kick_two = pull_momentum + step_size * grad_drift_two
    returning = jnp.concatenate([grad_drift_two, grad_kick_two], 0)
    sent_back = jnp.where(
        received[None] < particle_count,
        returning[:, jnp.minimum(received, particle_count - 1)],
        0.0,
    )
    sent_back = sent_back.reshape(6, 4, MOVE_MOST)
    homecoming = trade_pairs(sent_back[:, 0:2], sent_back[:, 2:4])
    returned = jnp.stack([homecoming[1], homecoming[0], homecoming[3], homecoming[2]], 1)
    gathered_home = jnp.where(destination[None] == 0, returning[:, slot_index], 0.0)
    home_spots = jnp.where(filled, chosen, particle_count).reshape(-1)
    gathered_home = gathered_home.at[:, home_spots].set(returned.reshape(6, -1), mode="drop")
    grad_drift_one = gathered_home[:3] + force_pullback(
        push_one, cell_first, drift_one, step_size * gathered_home[3:]
    )
    grad_momentum = gathered_home[3:] + step_size * grad_drift_one
    return (grad_drift_one, grad_momentum)


def solution(mesh):
    return jax.shard_map(
        local,
        mesh=mesh,
        in_specs=(
            P(None, ("gx", "gy")),
            P(None, ("gx", "gy")),
            P(None, ("gx", "gy")),
            P(None, ("gx", "gy")),
            P(("gx", "gy")),
            P(("gx", "gy")),
            P(None, ("gx", "gy")),
            P(None, ("gx", "gy")),
        ),
        out_specs=(P(None, ("gx", "gy")), P(None, ("gx", "gy"))),
        check_vma=False,
    )
```

profile of v0, /device:TPU:1, one launch (start us, length us, event | category | flops | bytes accessed | tf_op | source)
XLA Modules:
  0.0 329.2 jit_solution(8306297615378816670)
XLA Ops:
  1.4 1.0 maximum_subtract_fusion
  2.4 12.2 %while.91 = (s32[]{:T(128)}, f32[1,27,256]{2,1,0:T(8,128)S(1)}, s32[8,3,512]{2,1,0:T(4,128)}, f32[8,3,512]{2,1,0:T(4,128)S(1)}, s32[]{:T(128)}, /*index=5*/s32[]{:T(128)}, s32[]{}, s32[]{}) while((s32[]{:T(128)}, f32[1,27,256]{2,1,0:T(8,128)S(1)}, s32[8,3,512]{2,1,0:T(4,128)}, f32[8,3,512]{2,1,0:T(4,128)S(1)}, s32[]{:T(128)}, ...), condition=%wide.region_2.3_spmd.clone, body=%wide.region_1.2_spmd.clone.sunk | while | flops 43300868 | bytes 131215 | solution.py:80
  14.7 4.0 %collective-permute-start = (f32[1,9,2,256]{3,1,2,0:T(8,128)S(1)}, f32[1,9,2,256]{3,1,2,0:T(8,128)S(1)}, u32[]{:S(2)}, u32[]{:S(2)}) collective-permute-start(f32[1,9,2,256]{3,1,2,0:T(8,128)S(1)} %copy.330), channel_id=1, source_target_pairs={{0,8},{8,16},{16,24},{24,32},{32,40},{40,48},{48,56},{56,64},{64,7... | collective-permute-start | bytes 55304 | tf_op jit(solution)/shard_map/ppermute | solution.py:22
  18.7 7.8 %collective-permute-start.1 = (f32[1,9,2,256]{3,1,2,0:T(8,128)S(1)}, f32[1,9,2,256]{3,1,2,0:T(8,128)S(1)}, u32[]{:S(2)}, u32[]{:S(2)}) collective-permute-start(f32[1,9,2,256]{3,1,2,0:T(8,128)S(1)} %copy.334), channel_id=1, source_target_pairs={{8,0},{16,8},{24,16},{32,24},{40,32},{48,40},{56,48},{64,56},{72,6... | collective-permute-start | bytes 55304 | tf_op jit(solution)/shard_map/ppermute | solution.py:23
  28.8 5.8 %sort.17 = (s32[4096]{0:T(1024)}, s32[4096]{0:T(1024)S(1)}) sort(s32[4096]{0:T(1024)S(1)} %copy-done.3, s32[4096]{0:T(1024)S(1)} %iota.435), dimensions={0}, to_apply=%region_6.7 | sort | flops 49152 | bytes 65536 | tf_op jit(solution)/shard_map/jit(argsort)/sort | solution.py:183
  34.6 1.7 gather_fusion
  36.4 1.7 gather_fusion.1
  39.4 1.7 gather_fusion.2
  41.1 1.7 gather_fusion.3
  43.0 6.2 %gather_fusion.5 = s32[1024]{0:T(1024)S(1)} fusion(s32[4096]{0:T(1024)S(1)} %copy-done, s32[1024]{0:T(1024)S(1)} %broadcast_clamp_fusion.1), kind=kCustom, calls=%fused_computation.5 | custom fusion | bytes 12288 | tf_op jit(solution)/shard_map/gather | solution.py:227
  49.8 20.6 %all-gather = f32[72,5,256]{2,1,0:T(8,128)S(1)} all-gather(f32[9,5,256]{2,1,0:T(8,128)S(1)} %fusion.143), channel_id=2, replica_groups=mesh['gx'=64,'gy'=8] {'gy'}, dimensions={0}, use_global_device_ids=true | all-gather | bytes 414720 | tf_op jit(solution)/shard_map/all_gather | solution.py:150
  71.3 12.9 %while.88 = (s32[]{:T(128)}, f32[8,1,3,512]{3,2,1,0:T(4,128)S(1)}, s32[8,3,512]{2,1,0:T(4,128)}, f32[8,3,512]{2,1,0:T(4,128)S(1)}, f32[81,256]{1,0:T(8,128)S(1)}, /*index=5*/s32[]{:T(128)}, s32[]{:T(128)}, s32[]{}, s32[]{}) while((s32[]{:T(128)}, f32[8,1,3,512]{3,2,1,0:T(4,128)S(1)}, s32[8,3,512]{2,1,0:T(4,128)}, f32[8,3,512]{2,1,0:T(4,128)S(1)}, ...), condition=%wide.region_5.6_spmd, body=%wide.region_3.5_spmd.sunk | while | flops 128303104 | bytes 955537 | solution.py:110
  85.0 2.8 gather_fusion.4
  88.0 2.1 collective-permute-start.5
  90.1 4.4 %collective-permute-start.4 = (f32[7,1,256]{2,1,0:T(1,128)S(1)}, f32[7,1,256]{2,1,0:T(1,128)S(1)}, u32[]{:S(2)}, u32[]{:S(2)}) collective-permute-start(f32[7,1,256]{2,1,0:T(1,128)S(1)} %get-tuple-element.759), channel_id=1, source_target_pairs={{0,1},{1,2},{2,3},{3,4},{4,5},{5,6},{6,7},{7,0},{8,9},{9,10},{10,1... | collective-permute-start | bytes 21512 | tf_op jit(solution)/shard_map/ppermute | solution.py:22
  94.5 4.4 %collective-permute-start.3 = (f32[7,1,256]{2,1,0:T(1,128)S(1)}, f32[7,1,256]{2,1,0:T(1,128)S(1)}, u32[]{:S(2)}, u32[]{:S(2)}) collective-permute-start(f32[7,1,256]{2,1,0:T(1,128)S(1)} %get-tuple-element.757), channel_id=1, source_target_pairs={{8,0},{16,8},{24,16},{32,24},{40,32},{48,40},{56,48},{64,56},{72,6... | collective-permute-start | bytes 21512 | tf_op jit(solution)/shard_map/ppermute | solution.py:23
  98.9 1.9 collective-permute-start.2
  100.9 6.6 %collective-permute-done.2 = f32[7,1,256]{2,1,0:T(1,128)S(1)} collective-permute-done((f32[7,1,256]{2,1,0:T(1,128)S(1)}, f32[7,1,256]{2,1,0:T(1,128)S(1)}, u32[]{:S(2)}, u32[]{:S(2)}) %collective-permute-start.2) | collective-permute-done | bytes 7200 | tf_op jit(solution)/shard_map/ppermute | solution.py:22
  107.6 2.2 copy.281
  109.9 14.1 %scatter_custom_fusion = f32[6,4096]{0,1:T(8,128)S(1)} fusion(s32[5120]{0:T(1024)S(1)} %bitcast.436, f32[5120,6]{1,0:T(8,128)} %copy.281, f32[]{:T(128)} %constant.568.clone.1), kind=kCustom, calls=%fused_computation.335 | custom fusion | bytes 98816 | tf_op jit(solution)/shard_map/scatter | solution.py:240
  123.9 2.6 fusion.253
  126.6 2.4 copy.335
  129.6 12.2 %while.92 = (s32[]{:T(128)}, f32[1,27,256]{2,1,0:T(8,128)S(1)}, s32[8,3,512]{2,1,0:T(4,128)}, f32[8,3,512]{2,1,0:T(4,128)S(1)}, s32[]{:T(128)}, /*index=5*/s32[]{:T(128)}, s32[]{}, s32[]{}) while((s32[]{:T(128)}, f32[1,27,256]{2,1,0:T(8,128)S(1)}, s32[8,3,512]{2,1,0:T(4,128)}, f32[8,3,512]{2,1,0:T(4,128)S(1)}, s32[]{:T(128)}, ...), condition=%wide.region_10.11_spmd.clone, body=%wide.region_9.10_spmd.clone.sunk | while | flops 43300868 | bytes 131215 | solution.py:80
  141.9 13.4 %while.93 = (s32[]{:T(128)}, f32[3,27,256]{2,1,0:T(8,128)S(1)}, f32[8,3,512]{2,1,0:T(4,128)S(1)}, s32[8,3,512]{2,1,0:T(4,128)}, f32[8,3,512]{2,1,0:T(4,128)S(1)}, /*index=5*/s32[]{:T(128)}, s32[]{:T(128)}, s32[]{}, s32[]{}) while((s32[]{:T(128)}, f32[3,27,256]{2,1,0:T(8,128)S(1)}, f32[8,3,512]{2,1,0:T(4,128)S(1)}, ...), condition=%wide.region_12.13_spmd.clone, body=%wide.region_11.12_spmd.clone.sunk | while | flops 128304640 | bytes 370843 | solution.py:80
  155.4 1.9 collective-permute-start.6
  157.4 7.6 %collective-permute-start.7 = (f32[1,9,2,256]{3,1,2,0:T(8,128)S(1)}, f32[1,9,2,256]{3,1,2,0:T(8,128)S(1)}, u32[]{:S(2)}, u32[]{:S(2)}) collective-permute-start(f32[1,9,2,256]{3,1,2,0:T(8,128)S(1)} %copy.341), channel_id=1, source_target_pairs={{8,0},{16,8},{24,16},{32,24},{40,32},{48,40},{56,48},{64,56},{72,6... | collective-permute-start | bytes 55304 | tf_op jit(solution)/shard_map/ppermute | solution.py:23
  165.0 1.9 collective-permute-start.9
  166.9 7.6 %collective-permute-start.8 = (f32[3,9,2,256]{3,1,2,0:T(8,128)S(1)}, f32[3,9,2,256]{3,1,2,0:T(8,128)S(1)}, u32[]{:S(2)}, u32[]{:S(2)}) collective-permute-start(f32[3,9,2,256]{3,1,2,0:T(8,128)S(1)} %copy.344), channel_id=1, source_target_pairs={{8,0},{16,8},{24,16},{32,24},{40,32},{48,40},{56,48},{64,56},{72,6... | collective-permute-start | bytes 165896 | tf_op jit(solution)/shard_map/ppermute | solution.py:23
  175.0 18.5 %all-gather.1 = f32[72,5,256]{2,1,0:T(8,128)S(1)} all-gather(f32[9,5,256]{2,1,0:T(8,128)S(1)} %fusion.141), channel_id=3, replica_groups=mesh['gx'=64,'gy'=8] {'gy'}, dimensions={0}, use_global_device_ids=true | all-gather | bytes 414720 | tf_op jit(solution)/shard_map/all_gather | solution.py:150
  194.5 14.8 %all_gather.14 = f32[2,72,3,256]{3,0,2,1:T(2,128)S(1)} all-gather(f32[2,9,3,256]{3,0,2,1:T(2,128)S(1)} %copy.298), channel_id=1, replica_groups=mesh['gx'=64,'gy'=8] {'gy'}, dimensions={1}, use_global_device_ids=true | all-gather | bytes 497664 | tf_op jit(solution)/shard_map/all_gather | solution.py:150
  210.3 16.8 %while.89 = (s32[]{:T(128)}, f32[8,4,4,512]{3,2,1,0:T(4,128)S(1)}, s32[8,3,512]{2,1,0:T(4,128)}, f32[8,3,512]{2,1,0:T(4,128)S(1)}, f32[108,256]{1,0:T(8,128)S(1)}, /*index=5*/s32[]{:T(128)}, s32[]{:T(128)}, s32[]{}, s32[]{}) while((s32[]{:T(128)}, f32[8,4,4,512]{3,2,1,0:T(4,128)S(1)}, s32[8,3,512]{2,1,0:T(4,128)}, ...), condition=%wide.region_18.19_spmd, body=%wide.region_13.18_spmd.sunk | while | flops 341865984 | bytes 4495505 | solution.py:110
  228.1 2.8 gather_fusion.7
  231.2 2.2 collective-permute-start.10
  233.4 3.1 collective-permute-start.11
  236.5 2.6 collective-permute-start.12
  239.1 3.8 %collective-permute-start.13 = (f32[6,1,256]{2,1,0:T(1,128)S(1)}, f32[6,1,256]{2,1,0:T(1,128)S(1)}, u32[]{:S(2)}, u32[]{:S(2)}) collective-permute-start(f32[6,1,256]{2,1,0:T(1,128)S(1)} %get-tuple-element.771), channel_id=1, source_target_pairs={{0,1},{1,2},{2,3},{3,4},{4,5},{5,6},{6,7},{7,0},{8,9},{9,10},{10,1... | collective-permute-start | bytes 18440 | tf_op jit(solution)/shard_map/ppermute | solution.py:22
  243.0 14.1 %gather_fusion.6 = f32[4096,6]{1,0:T(8,128)} fusion(f32[6,4096]{0,1:T(8,128)S(1)} %copy.303, s32[4096]{0:T(1024)S(1)} %get-tuple-element.774), kind=kCustom, calls=%fused_computation.6 | custom fusion | bytes 212992 | tf_op jit(solution)/shard_map/gather | solution.py:257
  257.0 3.6 %select_bitcast_fusion = f32[6,4096]{0,1:T(8,128)S(1)} fusion(f32[4096,6]{1,0:T(8,128)} %gather_fusion.6, pred[4096]{0:T(1024)(128)(4,1)S(1)} %get-tuple-element.613), kind=kLoop, calls=%fused_computation.324 | loop fusion | flops 24576 | bytes 200704 | tf_op jit(solution)/shard_map/jit(_where)/select_n | solution.py:257
  260.9 4.1 %scatter_fusion = f32[6,4096]{0,1:T(8,128)S(1)} fusion(f32[6,4096]{0,1:T(8,128)S(1)} %select_bitcast_fusion, s32[1024]{0:T(1024)S(1)} %bitcast.437, f32[1024,6]{1,0:T(8,128)S(1)} %bitcast.352), kind=kCustom, calls=%fused_computation.9 | custom fusion | bytes 77824 | tf_op jit(solution)/shard_map/scatter | solution.py:259
  265.0 2.7 fusion.252
  267.7 2.2 copy.349
  270.0 13.4 %while.94 = (s32[]{:T(128)}, f32[3,27,256]{2,1,0:T(8,128)S(1)}, f32[8,3,512]{2,1,0:T(4,128)S(1)}, s32[8,3,512]{2,1,0:T(4,128)}, f32[8,3,512]{2,1,0:T(4,128)S(1)}, /*index=5*/s32[]{:T(128)}, s32[]{:T(128)}, s32[]{}, s32[]{}) while((s32[]{:T(128)}, f32[3,27,256]{2,1,0:T(8,128)S(1)}, f32[8,3,512]{2,1,0:T(4,128)S(1)}, ...), condition=%wide.region_22.23_spmd.clone, body=%wide.region_21.22_spmd.clone.sunk | while | flops 128304640 | bytes 370843 | solution.py:80
  270.0 0.9 dynamic-slice_add_fusion.20
  283.5 1.9 collective-permute-start.15
  285.5 7.6 %collective-permute-start.14 = (f32[3,9,2,256]{3,1,2,0:T(8,128)S(1)}, f32[3,9,2,256]{3,1,2,0:T(8,128)S(1)}, u32[]{:S(2)}, u32[]{:S(2)}) collective-permute-start(f32[3,9,2,256]{3,1,2,0:T(8,128)S(1)} %copy.352), channel_id=1, source_target_pairs={{8,0},{16,8},{24,16},{32,24},{40,32},{48,40},{56,48},{64,56},{72,6... | collective-permute-start | bytes 165896 | tf_op jit(solution)/shard_map/ppermute | solution.py:23
  294.2 1.2 collective-permute-done.14
  295.7 14.8 %all_gather.15 = f32[2,72,3,256]{3,0,2,1:T(2,128)S(1)} all-gather(f32[2,9,3,256]{3,0,2,1:T(2,128)S(1)} %copy.315), channel_id=1, replica_groups=mesh['gx'=64,'gy'=8] {'gy'}, dimensions={1}, use_global_device_ids=true | all-gather | bytes 497664 | tf_op jit(solution)/shard_map/all_gather | solution.py:150
  311.4 16.8 %while.90 = (s32[]{:T(128)}, f32[8,4,4,512]{3,2,1,0:T(4,128)S(1)}, s32[8,3,512]{2,1,0:T(4,128)}, f32[8,3,512]{2,1,0:T(4,128)S(1)}, f32[108,256]{1,0:T(8,128)S(1)}, /*index=5*/s32[]{:T(128)}, s32[]{:T(128)}, s32[]{}, s32[]{}) while((s32[]{:T(128)}, f32[8,4,4,512]{3,2,1,0:T(4,128)S(1)}, s32[8,3,512]{2,1,0:T(4,128)}, ...), condition=%wide.region_28.29_spmd, body=%wide.region_23.28_spmd.sunk | while | flops 341865984 | bytes 4495505 | solution.py:110
  (673 shorter events, 108.0 us)
Async XLA Ops:
  2.4 24.2 %copy-start.3 = (s32[4096]{0:T(1024)S(1)}, s32[4096]{0:T(1024)}, u32[]{:S(2)}) copy-start(s32[4096]{0:T(1024)} %param.26) | copy-start | bytes 49156
  14.7 34.7 %collective-permute-start = (f32[1,9,2,256]{3,1,2,0:T(8,128)S(1)}, f32[1,9,2,256]{3,1,2,0:T(8,128)S(1)}, u32[]{:S(2)}, u32[]{:S(2)}) collective-permute-start(f32[1,9,2,256]{3,1,2,0:T(8,128)S(1)} %copy.330), channel_id=1, source_target_pairs={{0,8},{8,16},{16,24},{24,32},{32,40},{40,48},{48,56},{56,64},{64,7... | collective-permute-start | bytes 55304 | tf_op jit(solution)/shard_map/ppermute | solution.py:22
  18.7 30.7 %collective-permute-start.1 = (f32[1,9,2,256]{3,1,2,0:T(8,128)S(1)}, f32[1,9,2,256]{3,1,2,0:T(8,128)S(1)}, u32[]{:S(2)}, u32[]{:S(2)}) collective-permute-start(f32[1,9,2,256]{3,1,2,0:T(8,128)S(1)} %copy.334), channel_id=1, source_target_pairs={{8,0},{16,8},{24,16},{32,24},{40,32},{48,40},{56,48},{64,56},{72,6... | collective-permute-start | bytes 55304 | tf_op jit(solution)/shard_map/ppermute | solution.py:23
  34.6 8.3 %copy-start = (s32[4096]{0:T(1024)S(1)}, s32[4096]{0:T(1024)}, u32[]{:S(2)}) copy-start(s32[4096]{0:T(1024)} %param.27) | copy-start | bytes 49156
  43.0 6.3 %copy-start.5 = (f32[3,4096]{1,0:T(4,128)S(1)}, f32[3,4096]{1,0:T(4,128)}, u32[]{:S(2)}) copy-start(f32[3,4096]{1,0:T(4,128)} %param.29) | copy-start | bytes 147460
  71.3 13.0 %copy-start.4 = (f32[3,4096]{1,0:T(4,128)S(1)}, f32[3,4096]{1,0:T(4,128)}, u32[]{:S(2)}) copy-start(f32[3,4096]{1,0:T(4,128)} %param.23) | copy-start | bytes 147460
  88.0 12.8 %collective-permute-start.5 = (f32[7,1,256]{2,1,0:T(1,128)S(1)}, f32[7,1,256]{2,1,0:T(1,128)S(1)}, u32[]{:S(2)}, u32[]{:S(2)}) collective-permute-start(f32[7,1,256]{2,1,0:T(1,128)S(1)} %get-tuple-element.758), channel_id=1, source_target_pairs={{1,0},{2,1},{3,2},{4,3},{5,4},{6,5},{7,6},{0,7},{9,8},{10,9},{11,1... | collective-permute-start | bytes 21512 | tf_op jit(solution)/shard_map/ppermute | solution.py:23
  90.1 10.8 %collective-permute-start.4 = (f32[7,1,256]{2,1,0:T(1,128)S(1)}, f32[7,1,256]{2,1,0:T(1,128)S(1)}, u32[]{:S(2)}, u32[]{:S(2)}) collective-permute-start(f32[7,1,256]{2,1,0:T(1,128)S(1)} %get-tuple-element.759), channel_id=1, source_target_pairs={{0,1},{1,2},{2,3},{3,4},{4,5},{5,6},{6,7},{7,0},{8,9},{9,10},{10,1... | collective-permute-start | bytes 21512 | tf_op jit(solution)/shard_map/ppermute | solution.py:22
  94.5 6.4 %collective-permute-start.3 = (f32[7,1,256]{2,1,0:T(1,128)S(1)}, f32[7,1,256]{2,1,0:T(1,128)S(1)}, u32[]{:S(2)}, u32[]{:S(2)}) collective-permute-start(f32[7,1,256]{2,1,0:T(1,128)S(1)} %get-tuple-element.757), channel_id=1, source_target_pairs={{8,0},{16,8},{24,16},{32,24},{40,32},{48,40},{56,48},{64,56},{72,6... | collective-permute-start | bytes 21512 | tf_op jit(solution)/shard_map/ppermute | solution.py:23
  98.9 8.6 %collective-permute-start.2 = (f32[7,1,256]{2,1,0:T(1,128)S(1)}, f32[7,1,256]{2,1,0:T(1,128)S(1)}, u32[]{:S(2)}, u32[]{:S(2)}) collective-permute-start(f32[7,1,256]{2,1,0:T(1,128)S(1)} %get-tuple-element.756), channel_id=1, source_target_pairs={{0,8},{8,16},{16,24},{24,32},{32,40},{40,48},{48,56},{56,64},{64,7... | collective-permute-start | bytes 21512 | tf_op jit(solution)/shard_map/ppermute | solution.py:22
  126.6 2.4 copy-start.2
  155.4 19.1 %collective-permute-start.6 = (f32[1,9,2,256]{3,1,2,0:T(8,128)S(1)}, f32[1,9,2,256]{3,1,2,0:T(8,128)S(1)}, u32[]{:S(2)}, u32[]{:S(2)}) collective-permute-start(f32[1,9,2,256]{3,1,2,0:T(8,128)S(1)} %copy.337), channel_id=1, source_target_pairs={{0,8},{8,16},{16,24},{24,32},{32,40},{40,48},{48,56},{56,64},{64,7... | collective-permute-start | bytes 55304 | tf_op jit(solution)/shard_map/ppermute | solution.py:22
  157.4 17.2 %collective-permute-start.7 = (f32[1,9,2,256]{3,1,2,0:T(8,128)S(1)}, f32[1,9,2,256]{3,1,2,0:T(8,128)S(1)}, u32[]{:S(2)}, u32[]{:S(2)}) collective-permute-start(f32[1,9,2,256]{3,1,2,0:T(8,128)S(1)} %copy.341), channel_id=1, source_target_pairs={{8,0},{16,8},{24,16},{32,24},{40,32},{48,40},{56,48},{64,56},{72,6... | collective-permute-start | bytes 55304 | tf_op jit(solution)/shard_map/ppermute | solution.py:23
  165.0 29.2 %collective-permute-start.9 = (f32[3,9,2,256]{3,1,2,0:T(8,128)S(1)}, f32[3,9,2,256]{3,1,2,0:T(8,128)S(1)}, u32[]{:S(2)}, u32[]{:S(2)}) collective-permute-start(f32[3,9,2,256]{3,1,2,0:T(8,128)S(1)} %copy.345), channel_id=1, source_target_pairs={{0,8},{8,16},{16,24},{24,32},{32,40},{40,48},{48,56},{56,64},{64,7... | collective-permute-start | bytes 165896 | tf_op jit(solution)/shard_map/ppermute | solution.py:22
  166.9 27.3 %collective-permute-start.8 = (f32[3,9,2,256]{3,1,2,0:T(8,128)S(1)}, f32[3,9,2,256]{3,1,2,0:T(8,128)S(1)}, u32[]{:S(2)}, u32[]{:S(2)}) collective-permute-start(f32[3,9,2,256]{3,1,2,0:T(8,128)S(1)} %copy.344), channel_id=1, source_target_pairs={{8,0},{16,8},{24,16},{32,24},{40,32},{48,40},{56,48},{64,56},{72,6... | collective-permute-start | bytes 165896 | tf_op jit(solution)/shard_map/ppermute | solution.py:23
  210.3 17.1 %copy-start.6 = (f32[3,4096]{1,0:T(4,128)S(1)}, f32[3,4096]{1,0:T(4,128)}, u32[]{:S(2)}) copy-start(f32[3,4096]{1,0:T(4,128)} %param.28) | copy-start | bytes 147460
  231.2 29.5 %collective-permute-start.10 = (f32[6,1,256]{2,1,0:T(1,128)S(1)}, f32[6,1,256]{2,1,0:T(1,128)S(1)}, u32[]{:S(2)}, u32[]{:S(2)}) collective-permute-start(f32[6,1,256]{2,1,0:T(1,128)S(1)} %get-tuple-element.770), channel_id=1, source_target_pairs={{8,0},{16,8},{24,16},{32,24},{40,32},{48,40},{56,48},{64,56},{72,6... | collective-permute-start | bytes 18440 | tf_op jit(solution)/shard_map/ppermute | solution.py:23
  233.4 27.3 %collective-permute-start.11 = (f32[6,1,256]{2,1,0:T(1,128)S(1)}, f32[6,1,256]{2,1,0:T(1,128)S(1)}, u32[]{:S(2)}, u32[]{:S(2)}) collective-permute-start(f32[6,1,256]{2,1,0:T(1,128)S(1)} %get-tuple-element.773), channel_id=1, source_target_pairs={{0,8},{8,16},{16,24},{24,32},{32,40},{40,48},{48,56},{56,64},{64,7... | collective-permute-start | bytes 18440 | tf_op jit(solution)/shard_map/ppermute | solution.py:22
  236.5 24.2 %collective-permute-start.12 = (f32[6,1,256]{2,1,0:T(1,128)S(1)}, f32[6,1,256]{2,1,0:T(1,128)S(1)}, u32[]{:S(2)}, u32[]{:S(2)}) collective-permute-start(f32[6,1,256]{2,1,0:T(1,128)S(1)} %get-tuple-element.772), channel_id=1, source_target_pairs={{1,0},{2,1},{3,2},{4,3},{5,4},{6,5},{7,6},{0,7},{9,8},{10,9},{11,1... | collective-permute-start | bytes 18440 | tf_op jit(solution)/shard_map/ppermute | solution.py:23
  239.1 21.6 %collective-permute-start.13 = (f32[6,1,256]{2,1,0:T(1,128)S(1)}, f32[6,1,256]{2,1,0:T(1,128)S(1)}, u32[]{:S(2)}, u32[]{:S(2)}) collective-permute-start(f32[6,1,256]{2,1,0:T(1,128)S(1)} %get-tuple-element.771), channel_id=1, source_target_pairs={{0,1},{1,2},{2,3},{3,4},{4,5},{5,6},{6,7},{7,0},{8,9},{9,10},{10,1... | collective-permute-start | bytes 18440 | tf_op jit(solution)/shard_map/ppermute | solution.py:22
  270.0 23.1 %copy-start.1 = (f32[3,4096]{0,1:T(8,128)S(1)}, f32[3,4096]{0,1:T(8,128)}, u32[]{:S(2)}) copy-start(f32[3,4096]{0,1:T(8,128)} %get-tuple-element.718) | copy-start | bytes 147460
  283.5 10.7 %collective-permute-start.15 = (f32[3,9,2,256]{3,1,2,0:T(8,128)S(1)}, f32[3,9,2,256]{3,1,2,0:T(8,128)S(1)}, u32[]{:S(2)}, u32[]{:S(2)}) collective-permute-start(f32[3,9,2,256]{3,1,2,0:T(8,128)S(1)} %copy.353), channel_id=1, source_target_pairs={{0,8},{8,16},{16,24},{24,32},{32,40},{40,48},{48,56},{56,64},{64,7... | collective-permute-start | bytes 165896 | tf_op jit(solution)/shard_map/ppermute | solution.py:22
  285.5 9.9 %collective-permute-start.14 = (f32[3,9,2,256]{3,1,2,0:T(8,128)S(1)}, f32[3,9,2,256]{3,1,2,0:T(8,128)S(1)}, u32[]{:S(2)}, u32[]{:S(2)}) collective-permute-start(f32[3,9,2,256]{3,1,2,0:T(8,128)S(1)} %copy.352), channel_id=1, source_target_pairs={{8,0},{16,8},{24,16},{32,24},{40,32},{48,40},{56,48},{64,56},{72,6... | collective-permute-start | bytes 165896 | tf_op jit(solution)/shard_map/ppermute | solution.py:23
where the time goes:
time: 334 us; the launch traced here: 329 us
  other arithmetic  71.1 us (21%)
  local copies, waits for them, and re-layouts  70.9 us (21%)
  blocking collectives  68.8 us (21%)
  starting transfers between devices  64.9 us (19%)
  matrix products  39.7 us (12%)
  waiting for transfers between devices  8.23 us (2%)
  loops' own time  3.7 us (1%)
    all_gather x4, blocking collectives, sum_lines(): gathered = lax.all_gather(field, 'gy', axis=1, tiled=True)  68.8 us
    add x56, other arithmetic, cloud_weights(): corner = (cell_block[1] * plane_count + cell_block[0])[None, :]  46.3 us
    ppermute x8, starting transfers between devices, with_halo(): after = lax.ppermute(first, axis, down)  41.8 us
    ppermute x8, starting transfers between devices, with_halo(): before = lax.ppermute(last, axis, up)  23 us
    dot_general x32, matrix products, add_block(): jnp.einsum('crb,zb->crz', spread, weights[3], precision=highest)  20.9 us
    dot_general x24, matrix products, one_block(): jnp.dot(flattened, columns, precision=highest, preferred_element_type=jnp...  15.9 us
    scatter x1, local copies, waits for them, and re-layouts, local(): arrived = jnp.zeros((6, particle_count), jnp.float32).at[:, placed].set(j...  14.1 us
    gather x1, local copies, waits for them, and re-layouts, local(): returning[:, slot_index]  14.1 us
  transfers between devices with their start and end apart: 16, of which 3 were waited for; matrix products, arithmetic and copies ran while one was open for 13% of the time, Pallas kernels for 0%

commit v1 on v0

--- a/solution.py
+++ b/solution.py
@@ -147,7 +147,9 @@
     anchor = lax.axis_index("gy") * own_rows
     targets = (anchor + jnp.arange(-1, own_rows + 2, dtype=jnp.int32)) % extent
     initial = jnp.zeros((field.shape[0], own_rows + 3, field.shape[2], field.shape[3]), jnp.float32)
-    gathered = lax.all_gather(field, "gy", axis=1, tiled=True)
+    gathered = jnp.concatenate(
+        lax.all_to_all(jnp.stack([field] * lax.axis_size("gy")), "gy", 0, 0), axis=1
+    )
     length = gathered.shape[1]
     positions = jnp.arange(length, dtype=jnp.int32)
     sources = (positions // band_rows * own_rows + positions % band_rows) % extent

time: 334 us -> 349 us (1.045)
  the two profiles are of different devices: /device:TPU:1 before, /device:TPU:62 now
where the time goes in v1:
time: 349 us; the launch traced here: 344 us
  starting transfers between devices  81.7 us (23%)
  local copies, waits for them, and re-layouts  74.8 us (21%)
  waiting for transfers between devices  71.3 us (20%)
  other arithmetic  71.2 us (20%)
  matrix products  39.8 us (11%)
  loops' own time  3.7 us (1%)
    all_to_all x4, waiting for transfers between devices, sum_lines(): lax.all_to_all(jnp.stack([field] * lax.axis_size('gy')), 'gy', 0, 0)  54.8 us
    add x56, other arithmetic, cloud_weights(): corner = (cell_block[1] * plane_count + cell_block[0])[None, :]  46.2 us
    ppermute x8, starting transfers between devices, with_halo(): before = lax.ppermute(last, axis, up)  43.8 us
    dot_general x32, matrix products, add_block(): jnp.einsum('crb,zb->crz', spread, weights[3], precision=highest)  20.9 us
    all_to_all x4, starting transfers between devices, sum_lines(): lax.all_to_all(jnp.stack([field] * lax.axis_size('gy')), 'gy', 0, 0)  20.7 us
    ppermute x8, starting transfers between devices, with_halo(): after = lax.ppermute(first, axis, down)  17.2 us
    dot_general x24, matrix products, one_block(): jnp.dot(flattened, columns, precision=highest, preferred_element_type=jnp...  15.9 us
    ppermute x8, waiting for transfers between devices, with_halo(): after = lax.ppermute(first, axis, down)  14.2 us
  transfers between devices with their start and end apart: 20, of which 8 were waited for; matrix products, arithmetic and copies ran while one was open for 13% of the time, Pallas kernels for 0%

profile of v1, /device:TPU:62, one launch (start us, length us, event | category | flops | bytes accessed | tf_op | source)
XLA Modules:
  0.0 344.2 jit_solution(17737706330056145744)
XLA Ops:
  2.4 12.2 %while.91 = (s32[]{:T(128)}, f32[1,27,256]{2,1,0:T(8,128)S(1)}, s32[8,3,512]{2,1,0:T(4,128)}, f32[8,3,512]{2,1,0:T(4,128)S(1)}, s32[]{:T(128)}, /*index=5*/s32[]{:T(128)}, s32[]{}, s32[]{}) while((s32[]{:T(128)}, f32[1,27,256]{2,1,0:T(8,128)S(1)}, s32[8,3,512]{2,1,0:T(4,128)}, f32[8,3,512]{2,1,0:T(4,128)S(1)}, s32[]{:T(128)}, ...), condition=%wide.region_2.3_spmd.clone, body=%wide.region_1.2_spmd.clone.sunk | while | flops 43300868 | bytes 131215 | solution.py:80
  14.6 3.4 collective-permute-start
  18.0 2.4 collective-permute-start.1
  22.2 5.8 %sort.17 = (s32[4096]{0:T(1024)}, s32[4096]{0:T(1024)S(1)}) sort(s32[4096]{0:T(1024)S(1)} %copy-done.3, s32[4096]{0:T(1024)S(1)} %iota.435), dimensions={0}, to_apply=%region_6.7 | sort | flops 49152 | bytes 65536 | tf_op jit(solution)/shard_map/jit(argsort)/sort | solution.py:185
  28.6 1.7 gather_fusion
  32.8 1.7 gather_fusion.2
  37.0 6.2 %gather_fusion.5 = s32[1024]{0:T(1024)S(1)} fusion(s32[4096]{0:T(1024)S(1)} %copy-done, s32[1024]{0:T(1024)S(1)} %broadcast_clamp_fusion.1), kind=kCustom, calls=%fused_computation.5 | custom fusion | bytes 12288 | tf_op jit(solution)/shard_map/gather | solution.py:229
  44.8 10.3 %all-to-all-start = ((f32[8,1,9,5,256]{4,1,3,2,0:T(1,128)}), f32[8,1,9,5,256]{4,1,3,2,0:T(1,128)S(1)}, u32[]{:S(2)}, u32[]{:S(2)}) async-start(f32[8,1,9,5,256]{4,1,3,2,0:T(1,128)} %stack.129), calls=%async_computation | async-start | bytes 737280 | tf_op jit(solution)/shard_map/all_to_all | solution.py:151
  55.2 15.0 %all-to-all-done = f32[8,1,9,5,256]{4,1,3,2,0:T(1,128)S(1)} async-done(((f32[8,1,9,5,256]{4,1,3,2,0:T(1,128)}), f32[8,1,9,5,256]{4,1,3,2,0:T(1,128)S(1)}, u32[]{:S(2)}, u32[]{:S(2)}) %all-to-all-start) | async-done | bytes 368672 | tf_op jit(solution)/shard_map/all_to_all | solution.py:151
  71.1 13.0 %while.88 = (s32[]{:T(128)}, f32[8,1,3,512]{3,2,1,0:T(4,128)S(1)}, s32[8,3,512]{2,1,0:T(4,128)}, f32[8,3,512]{2,1,0:T(4,128)S(1)}, f32[81,256]{1,0:T(8,128)S(1)}, /*index=5*/s32[]{:T(128)}, s32[]{:T(128)}, s32[]{}, s32[]{}) while((s32[]{:T(128)}, f32[8,1,3,512]{3,2,1,0:T(4,128)S(1)}, s32[8,3,512]{2,1,0:T(4,128)}, f32[8,3,512]{2,1,0:T(4,128)S(1)}, ...), condition=%wide.region_5.6_spmd, body=%wide.region_3.5_spmd.sunk | while | flops 128303104 | bytes 955537 | solution.py:110
  84.8 2.8 gather_fusion.4
  87.8 1.9 collective-permute-start.5
  89.7 2.4 collective-permute-start.4
  92.2 3.3 collective-permute-start.3
  95.4 6.8 %collective-permute-start.2 = (f32[7,1,256]{2,1,0:T(1,128)S(1)}, f32[7,1,256]{2,1,0:T(1,128)S(1)}, u32[]{:S(2)}, u32[]{:S(2)}) collective-permute-start(f32[7,1,256]{2,1,0:T(1,128)S(1)} %get-tuple-element.766), channel_id=1, source_target_pairs={{0,8},{8,16},{16,24},{24,32},{32,40},{40,48},{48,56},{56,64},{64,7... | collective-permute-start | bytes 21512 | tf_op jit(solution)/shard_map/ppermute | solution.py:22
  103.6 2.3 copy.298
  105.9 14.1 %scatter_custom_fusion = f32[6,4096]{0,1:T(8,128)S(1)} fusion(s32[5120]{0:T(1024)S(1)} %bitcast.452, f32[5120,6]{1,0:T(8,128)} %copy.298, f32[]{:T(128)} %constant.568.clone.1), kind=kCustom, calls=%fused_computation.335 | custom fusion | bytes 98816 | tf_op jit(solution)/shard_map/scatter | solution.py:242
  120.0 2.6 fusion.253
  122.6 2.4 copy.346
  125.7 13.3 %while.93 = (s32[]{:T(128)}, f32[3,27,256]{2,1,0:T(8,128)S(1)}, f32[8,3,512]{2,1,0:T(4,128)S(1)}, s32[8,3,512]{2,1,0:T(4,128)}, f32[8,3,512]{2,1,0:T(4,128)S(1)}, /*index=5*/s32[]{:T(128)}, s32[]{:T(128)}, s32[]{}, s32[]{}) while((s32[]{:T(128)}, f32[3,27,256]{2,1,0:T(8,128)S(1)}, f32[8,3,512]{2,1,0:T(4,128)S(1)}, ...), condition=%wide.region_12.13_spmd.clone, body=%wide.region_11.12_spmd.clone.sunk | while | flops 128304640 | bytes 370843 | solution.py:80
  139.2 12.2 %while.92 = (s32[]{:T(128)}, f32[1,27,256]{2,1,0:T(8,128)S(1)}, s32[8,3,512]{2,1,0:T(4,128)}, f32[8,3,512]{2,1,0:T(4,128)S(1)}, s32[]{:T(128)}, /*index=5*/s32[]{:T(128)}, s32[]{}, s32[]{}) while((s32[]{:T(128)}, f32[1,27,256]{2,1,0:T(8,128)S(1)}, s32[8,3,512]{2,1,0:T(4,128)}, f32[8,3,512]{2,1,0:T(4,128)S(1)}, s32[]{:T(128)}, ...), condition=%wide.region_10.11_spmd.clone, body=%wide.region_9.10_spmd.clone.sunk | while | flops 43300868 | bytes 131215 | solution.py:80
  151.4 8.4 %collective-permute-start.6 = (f32[1,9,2,256]{3,2,1,0:T(2,128)S(1)}, f32[1,9,2,256]{3,2,1,0:T(2,128)S(1)}, u32[]{:S(2)}, u32[]{:S(2)}) collective-permute-start(f32[1,9,2,256]{3,2,1,0:T(2,128)S(1)} %get-tuple-element.760), channel_id=1, source_target_pairs={{0,8},{8,16},{16,24},{24,32},{32,40},{40,48},{48,56},{56,64},{64,7... | collective-permute-start | bytes 55304 | tf_op jit(solution)/shard_map/ppermute | solution.py:22
  159.8 1.9 collective-permute-start.7
  161.8 8.1 %collective-permute-start.9 = (f32[3,9,2,256]{3,1,2,0:T(8,128)S(1)}, f32[3,9,2,256]{3,1,2,0:T(8,128)S(1)}, u32[]{:S(2)}, u32[]{:S(2)}) collective-permute-start(f32[3,9,2,256]{3,1,2,0:T(8,128)S(1)} %copy.351), channel_id=1, source_target_pairs={{0,8},{8,16},{16,24},{24,32},{32,40},{40,48},{48,56},{56,64},{64,7... | collective-permute-start | bytes 165896 | tf_op jit(solution)/shard_map/ppermute | solution.py:22
  170.0 1.9 collective-permute-start.8
  173.4 3.4 %all-to-all-start.1 = ((f32[8,1,9,5,256]{4,1,3,2,0:T(1,128)}), f32[8,1,9,5,256]{4,1,3,2,0:T(1,128)S(1)}, u32[]{:S(2)}, u32[]{:S(2)}) async-start(f32[8,1,9,5,256]{4,1,3,2,0:T(1,128)} %stack.135), calls=%async_computation.1 | async-start | bytes 737280 | tf_op jit(solution)/shard_map/all_to_all | solution.py:151
  176.9 3.9 %collective-permute-done.8 = f32[3,9,2,256]{3,1,2,0:T(8,128)S(1)} collective-permute-done((f32[3,9,2,256]{3,1,2,0:T(8,128)S(1)}, f32[3,9,2,256]{3,1,2,0:T(8,128)S(1)}, u32[]{:S(2)}, u32[]{:S(2)}) %collective-permute-start.8) | collective-permute-done | bytes 55328 | tf_op jit(solution)/shard_map/ppermute | solution.py:23
  181.1 10.7 %all-to-all-done.1 = f32[8,1,9,5,256]{4,1,3,2,0:T(1,128)S(1)} async-done(((f32[8,1,9,5,256]{4,1,3,2,0:T(1,128)}), f32[8,1,9,5,256]{4,1,3,2,0:T(1,128)S(1)}, u32[]{:S(2)}, u32[]{:S(2)}) %all-to-all-start.1) | async-done | bytes 368672 | tf_op jit(solution)/shard_map/all_to_all | solution.py:151
  192.7 3.5 %all-to-all-start.2 = ((f32[8,2,9,3,256]{4,1,3,2,0:T(2,128)}), f32[8,2,9,3,256]{4,1,3,2,0:T(2,128)S(1)}, u32[]{:S(2)}, u32[]{:S(2)}) async-start(f32[8,2,9,3,256]{4,1,3,2,0:T(2,128)} %stack.136), calls=%async_computation.2 | async-start | bytes 884736 | tf_op jit(solution)/shard_map/all_to_all | solution.py:151
  196.9 15.1 %all-to-all-done.2 = f32[8,2,9,3,256]{4,1,3,2,0:T(2,128)S(1)} async-done(((f32[8,2,9,3,256]{4,1,3,2,0:T(2,128)}), f32[8,2,9,3,256]{4,1,3,2,0:T(2,128)S(1)}, u32[]{:S(2)}, u32[]{:S(2)}) %all-to-all-start.2) | async-done | bytes 442400 | tf_op jit(solution)/shard_map/all_to_all | solution.py:151
  213.0 16.8 %while.89 = (s32[]{:T(128)}, f32[8,4,4,512]{3,2,1,0:T(4,128)S(1)}, s32[8,3,512]{2,1,0:T(4,128)}, f32[8,3,512]{2,1,0:T(4,128)S(1)}, f32[108,256]{1,0:T(8,128)S(1)}, /*index=5*/s32[]{:T(128)}, s32[]{:T(128)}, s32[]{}, s32[]{}) while((s32[]{:T(128)}, f32[8,4,4,512]{3,2,1,0:T(4,128)S(1)}, s32[8,3,512]{2,1,0:T(4,128)}, ...), condition=%wide.region_18.19_spmd, body=%wide.region_13.18_spmd.sunk | while | flops 341865984 | bytes 4495505 | solution.py:110
  230.8 2.8 gather_fusion.7
  233.9 1.9 collective-permute-start.10
  235.8 8.1 %collective-permute-start.11 = (f32[6,1,256]{2,1,0:T(1,128)S(1)}, f32[6,1,256]{2,1,0:T(1,128)S(1)}, u32[]{:S(2)}, u32[]{:S(2)}) collective-permute-start(f32[6,1,256]{2,1,0:T(1,128)S(1)} %get-tuple-element.773), channel_id=1, source_target_pairs={{0,8},{8,16},{16,24},{24,32},{32,40},{40,48},{48,56},{56,64},{64,7... | collective-permute-start | bytes 18440 | tf_op jit(solution)/shard_map/ppermute | solution.py:22
  244.0 1.9 collective-permute-start.12
  245.9 2.4 collective-permute-start.13
  248.3 14.1 %gather_fusion.6 = f32[4096,6]{1,0:T(8,128)} fusion(f32[6,4096]{0,1:T(8,128)S(1)} %copy.319, s32[4096]{0:T(1024)S(1)} %get-tuple-element.778), kind=kCustom, calls=%fused_computation.6 | custom fusion | bytes 212992 | tf_op jit(solution)/shard_map/gather | solution.py:259
  262.4 3.6 %select_bitcast_fusion = f32[6,4096]{0,1:T(8,128)S(1)} fusion(f32[4096,6]{1,0:T(8,128)} %gather_fusion.6, pred[4096]{0:T(1024)(128)(4,1)S(1)} %get-tuple-element.613), kind=kLoop, calls=%fused_computation.324 | loop fusion | flops 24576 | bytes 200704 | tf_op jit(solution)/shard_map/jit(_where)/select_n | solution.py:259
  266.3 4.1 %scatter_fusion = f32[6,4096]{0,1:T(8,128)S(1)} fusion(f32[6,4096]{0,1:T(8,128)S(1)} %select_bitcast_fusion, s32[1024]{0:T(1024)S(1)} %bitcast.453, f32[1024,6]{1,0:T(8,128)S(1)} %bitcast.368), kind=kCustom, calls=%fused_computation.9 | custom fusion | bytes 77824 | tf_op jit(solution)/shard_map/scatter | solution.py:261
  270.4 2.7 fusion.252
  273.1 2.2 copy.355
  275.3 13.4 %while.94 = (s32[]{:T(128)}, f32[3,27,256]{2,1,0:T(8,128)S(1)}, f32[8,3,512]{2,1,0:T(4,128)S(1)}, s32[8,3,512]{2,1,0:T(4,128)}, f32[8,3,512]{2,1,0:T(4,128)S(1)}, /*index=5*/s32[]{:T(128)}, s32[]{:T(128)}, s32[]{}, s32[]{}) while((s32[]{:T(128)}, f32[3,27,256]{2,1,0:T(8,128)S(1)}, f32[8,3,512]{2,1,0:T(4,128)S(1)}, ...), condition=%wide.region_22.23_spmd.clone, body=%wide.region_21.22_spmd.clone.sunk | while | flops 128304640 | bytes 370843 | solution.py:80
  288.8 4.0 %collective-permute-start.15 = (f32[3,9,2,256]{3,1,2,0:T(8,128)S(1)}, f32[3,9,2,256]{3,1,2,0:T(8,128)S(1)}, u32[]{:S(2)}, u32[]{:S(2)}) collective-permute-start(f32[3,9,2,256]{3,1,2,0:T(8,128)S(1)} %copy.359), channel_id=1, source_target_pairs={{0,8},{8,16},{16,24},{24,32},{32,40},{40,48},{48,56},{56,64},{64,7... | collective-permute-start | bytes 165896 | tf_op jit(solution)/shard_map/ppermute | solution.py:22
  293.0 1.9 collective-permute-start.14
  295.9 10.3 %collective-permute-done.14 = f32[3,9,2,256]{3,1,2,0:T(8,128)S(1)} collective-permute-done((f32[3,9,2,256]{3,1,2,0:T(8,128)S(1)}, f32[3,9,2,256]{3,1,2,0:T(8,128)S(1)}, u32[]{:S(2)}, u32[]{:S(2)}) %collective-permute-start.14) | collective-permute-done | bytes 55328 | tf_op jit(solution)/shard_map/ppermute | solution.py:23
  307.4 3.5 %all-to-all-start.3 = ((f32[8,2,9,3,256]{4,1,3,2,0:T(2,128)}), f32[8,2,9,3,256]{4,1,3,2,0:T(2,128)S(1)}, u32[]{:S(2)}, u32[]{:S(2)}) async-start(f32[8,2,9,3,256]{4,1,3,2,0:T(2,128)} %stack.143), calls=%async_computation.3 | async-start | bytes 884736 | tf_op jit(solution)/shard_map/all_to_all | solution.py:151
  311.5 14.0 %all-to-all-done.3 = f32[8,2,9,3,256]{4,1,3,2,0:T(2,128)S(1)} async-done(((f32[8,2,9,3,256]{4,1,3,2,0:T(2,128)}), f32[8,2,9,3,256]{4,1,3,2,0:T(2,128)S(1)}, u32[]{:S(2)}, u32[]{:S(2)}) %all-to-all-start.3) | async-done | bytes 442400 | tf_op jit(solution)/shard_map/all_to_all | solution.py:151
  326.4 16.8 %while.90 = (s32[]{:T(128)}, f32[8,4,4,512]{3,2,1,0:T(4,128)S(1)}, s32[8,3,512]{2,1,0:T(4,128)}, f32[8,3,512]{2,1,0:T(4,128)S(1)}, f32[108,256]{1,0:T(8,128)S(1)}, /*index=5*/s32[]{:T(128)}, s32[]{:T(128)}, s32[]{}, s32[]{}) while((s32[]{:T(128)}, f32[8,4,4,512]{3,2,1,0:T(4,128)S(1)}, s32[8,3,512]{2,1,0:T(4,128)}, ...), condition=%wide.region_28.29_spmd, body=%wide.region_23.28_spmd.sunk | while | flops 341865984 | bytes 4495505 | solution.py:110
  (673 shorter events, 119.0 us)
Async XLA Ops:
  2.4 18.1 %copy-start.3 = (s32[4096]{0:T(1024)S(1)}, s32[4096]{0:T(1024)}, u32[]{:S(2)}) copy-start(s32[4096]{0:T(1024)} %param.26) | copy-start | bytes 49156
  14.6 28.8 %collective-permute-start = (f32[1,9,2,256]{3,2,1,0:T(2,128)S(1)}, f32[1,9,2,256]{3,2,1,0:T(2,128)S(1)}, u32[]{:S(2)}, u32[]{:S(2)}) collective-permute-start(f32[1,9,2,256]{3,2,1,0:T(2,128)S(1)} %get-tuple-element.765), channel_id=1, source_target_pairs={{0,8},{8,16},{16,24},{24,32},{32,40},{40,48},{48,56},{56,64},{64,7... | collective-permute-start | bytes 55304 | tf_op jit(solution)/shard_map/ppermute | solution.py:22
  18.0 25.4 %collective-permute-start.1 = (f32[1,9,2,256]{3,2,1,0:T(2,128)S(1)}, f32[1,9,2,256]{3,2,1,0:T(2,128)S(1)}, u32[]{:S(2)}, u32[]{:S(2)}) collective-permute-start(f32[1,9,2,256]{3,2,1,0:T(2,128)S(1)} %get-tuple-element.764), channel_id=1, source_target_pairs={{8,0},{16,8},{24,16},{32,24},{40,32},{48,40},{56,48},{64,56},{72,6... | collective-permute-start | bytes 55304 | tf_op jit(solution)/shard_map/ppermute | solution.py:23
  28.6 8.4 %copy-start = (s32[4096]{0:T(1024)S(1)}, s32[4096]{0:T(1024)}, u32[]{:S(2)}) copy-start(s32[4096]{0:T(1024)} %param.27) | copy-start | bytes 49156
  37.0 18.1 %copy-start.5 = (f32[3,4096]{1,0:T(4,128)S(1)}, f32[3,4096]{1,0:T(4,128)}, u32[]{:S(2)}) copy-start(f32[3,4096]{1,0:T(4,128)} %param.29) | copy-start | bytes 147460
  44.8 25.3 %all-to-all-start = ((f32[8,1,9,5,256]{4,1,3,2,0:T(1,128)}), f32[8,1,9,5,256]{4,1,3,2,0:T(1,128)S(1)}, u32[]{:S(2)}, u32[]{:S(2)}) async-start(f32[8,1,9,5,256]{4,1,3,2,0:T(1,128)} %stack.129), calls=%async_computation | async-start | bytes 737280 | tf_op jit(solution)/shard_map/all_to_all | solution.py:151
  71.1 13.0 %copy-start.4 = (f32[3,4096]{1,0:T(4,128)S(1)}, f32[3,4096]{1,0:T(4,128)}, u32[]{:S(2)}) copy-start(f32[3,4096]{1,0:T(4,128)} %param.23) | copy-start | bytes 147460
  87.8 14.5 %collective-permute-start.5 = (f32[7,1,256]{2,1,0:T(1,128)S(1)}, f32[7,1,256]{2,1,0:T(1,128)S(1)}, u32[]{:S(2)}, u32[]{:S(2)}) collective-permute-start(f32[7,1,256]{2,1,0:T(1,128)S(1)} %get-tuple-element.768), channel_id=1, source_target_pairs={{1,0},{2,1},{3,2},{4,3},{5,4},{6,5},{7,6},{0,7},{9,8},{10,9},{11,1... | collective-permute-start | bytes 21512 | tf_op jit(solution)/shard_map/ppermute | solution.py:23
  89.7 12.6 %collective-permute-start.4 = (f32[7,1,256]{2,1,0:T(1,128)S(1)}, f32[7,1,256]{2,1,0:T(1,128)S(1)}, u32[]{:S(2)}, u32[]{:S(2)}) collective-permute-start(f32[7,1,256]{2,1,0:T(1,128)S(1)} %get-tuple-element.769), channel_id=1, source_target_pairs={{0,1},{1,2},{2,3},{3,4},{4,5},{5,6},{6,7},{7,0},{8,9},{9,10},{10,1... | collective-permute-start | bytes 21512 | tf_op jit(solution)/shard_map/ppermute | solution.py:22
  92.2 10.2 %collective-permute-start.3 = (f32[7,1,256]{2,1,0:T(1,128)S(1)}, f32[7,1,256]{2,1,0:T(1,128)S(1)}, u32[]{:S(2)}, u32[]{:S(2)}) collective-permute-start(f32[7,1,256]{2,1,0:T(1,128)S(1)} %get-tuple-element.767), channel_id=1, source_target_pairs={{8,0},{16,8},{24,16},{32,24},{40,32},{48,40},{56,48},{64,56},{72,6... | collective-permute-start | bytes 21512 | tf_op jit(solution)/shard_map/ppermute | solution.py:23
  95.4 8.1 %collective-permute-start.2 = (f32[7,1,256]{2,1,0:T(1,128)S(1)}, f32[7,1,256]{2,1,0:T(1,128)S(1)}, u32[]{:S(2)}, u32[]{:S(2)}) collective-permute-start(f32[7,1,256]{2,1,0:T(1,128)S(1)} %get-tuple-element.766), channel_id=1, source_target_pairs={{0,8},{8,16},{16,24},{24,32},{32,40},{40,48},{48,56},{56,64},{64,7... | collective-permute-start | bytes 21512 | tf_op jit(solution)/shard_map/ppermute | solution.py:22
  122.6 2.4 copy-start.2
  151.4 20.5 %collective-permute-start.6 = (f32[1,9,2,256]{3,2,1,0:T(2,128)S(1)}, f32[1,9,2,256]{3,2,1,0:T(2,128)S(1)}, u32[]{:S(2)}, u32[]{:S(2)}) collective-permute-start(f32[1,9,2,256]{3,2,1,0:T(2,128)S(1)} %get-tuple-element.760), channel_id=1, source_target_pairs={{0,8},{8,16},{16,24},{24,32},{32,40},{40,48},{48,56},{56,64},{64,7... | collective-permute-start | bytes 55304 | tf_op jit(solution)/shard_map/ppermute | solution.py:22
  159.8 12.1 %collective-permute-start.7 = (f32[1,9,2,256]{3,2,1,0:T(2,128)S(1)}, f32[1,9,2,256]{3,2,1,0:T(2,128)S(1)}, u32[]{:S(2)}, u32[]{:S(2)}) collective-permute-start(f32[1,9,2,256]{3,2,1,0:T(2,128)S(1)} %get-tuple-element.759), channel_id=1, source_target_pairs={{8,0},{16,8},{24,16},{32,24},{40,32},{48,40},{56,48},{64,56},{72,6... | collective-permute-start | bytes 55304 | tf_op jit(solution)/shard_map/ppermute | solution.py:23
  161.8 15.1 %collective-permute-start.9 = (f32[3,9,2,256]{3,1,2,0:T(8,128)S(1)}, f32[3,9,2,256]{3,1,2,0:T(8,128)S(1)}, u32[]{:S(2)}, u32[]{:S(2)}) collective-permute-start(f32[3,9,2,256]{3,1,2,0:T(8,128)S(1)} %copy.351), channel_id=1, source_target_pairs={{0,8},{8,16},{16,24},{24,32},{32,40},{40,48},{48,56},{56,64},{64,7... | collective-permute-start | bytes 165896 | tf_op jit(solution)/shard_map/ppermute | solution.py:22
  170.0 10.8 %collective-permute-start.8 = (f32[3,9,2,256]{3,1,2,0:T(8,128)S(1)}, f32[3,9,2,256]{3,1,2,0:T(8,128)S(1)}, u32[]{:S(2)}, u32[]{:S(2)}) collective-permute-start(f32[3,9,2,256]{3,1,2,0:T(8,128)S(1)} %copy.350), channel_id=1, source_target_pairs={{8,0},{16,8},{24,16},{32,24},{40,32},{48,40},{56,48},{64,56},{72,6... | collective-permute-start | bytes 165896 | tf_op jit(solution)/shard_map/ppermute | solution.py:23
  173.4 18.4 %all-to-all-start.1 = ((f32[8,1,9,5,256]{4,1,3,2,0:T(1,128)}), f32[8,1,9,5,256]{4,1,3,2,0:T(1,128)S(1)}, u32[]{:S(2)}, u32[]{:S(2)}) async-start(f32[8,1,9,5,256]{4,1,3,2,0:T(1,128)} %stack.135), calls=%async_computation.1 | async-start | bytes 737280 | tf_op jit(solution)/shard_map/all_to_all | solution.py:151
  192.7 19.4 %all-to-all-start.2 = ((f32[8,2,9,3,256]{4,1,3,2,0:T(2,128)}), f32[8,2,9,3,256]{4,1,3,2,0:T(2,128)S(1)}, u32[]{:S(2)}, u32[]{:S(2)}) async-start(f32[8,2,9,3,256]{4,1,3,2,0:T(2,128)} %stack.136), calls=%async_computation.2 | async-start | bytes 884736 | tf_op jit(solution)/shard_map/all_to_all | solution.py:151
  213.0 17.1 %copy-start.6 = (f32[3,4096]{1,0:T(4,128)S(1)}, f32[3,4096]{1,0:T(4,128)}, u32[]{:S(2)}) copy-start(f32[3,4096]{1,0:T(4,128)} %param.28) | copy-start | bytes 147460
  233.9 32.1 %collective-permute-start.10 = (f32[6,1,256]{2,1,0:T(1,128)S(1)}, f32[6,1,256]{2,1,0:T(1,128)S(1)}, u32[]{:S(2)}, u32[]{:S(2)}) collective-permute-start(f32[6,1,256]{2,1,0:T(1,128)S(1)} %get-tuple-element.770), channel_id=1, source_target_pairs={{8,0},{16,8},{24,16},{32,24},{40,32},{48,40},{56,48},{64,56},{72,6... | collective-permute-start | bytes 18440 | tf_op jit(solution)/shard_map/ppermute | solution.py:23
  235.8 30.2 %collective-permute-start.11 = (f32[6,1,256]{2,1,0:T(1,128)S(1)}, f32[6,1,256]{2,1,0:T(1,128)S(1)}, u32[]{:S(2)}, u32[]{:S(2)}) collective-permute-start(f32[6,1,256]{2,1,0:T(1,128)S(1)} %get-tuple-element.773), channel_id=1, source_target_pairs={{0,8},{8,16},{16,24},{24,32},{32,40},{40,48},{48,56},{56,64},{64,7... | collective-permute-start | bytes 18440 | tf_op jit(solution)/shard_map/ppermute | solution.py:22
  244.0 22.1 %collective-permute-start.12 = (f32[6,1,256]{2,1,0:T(1,128)S(1)}, f32[6,1,256]{2,1,0:T(1,128)S(1)}, u32[]{:S(2)}, u32[]{:S(2)}) collective-permute-start(f32[6,1,256]{2,1,0:T(1,128)S(1)} %get-tuple-element.772), channel_id=1, source_target_pairs={{1,0},{2,1},{3,2},{4,3},{5,4},{6,5},{7,6},{0,7},{9,8},{10,9},{11,1... | collective-permute-start | bytes 18440 | tf_op jit(solution)/shard_map/ppermute | solution.py:23
  245.9 20.2 %collective-permute-start.13 = (f32[6,1,256]{2,1,0:T(1,128)S(1)}, f32[6,1,256]{2,1,0:T(1,128)S(1)}, u32[]{:S(2)}, u32[]{:S(2)}) collective-permute-start(f32[6,1,256]{2,1,0:T(1,128)S(1)} %get-tuple-element.771), channel_id=1, source_target_pairs={{0,1},{1,2},{2,3},{3,4},{4,5},{5,6},{6,7},{7,0},{8,9},{9,10},{10,1... | collective-permute-start | bytes 18440 | tf_op jit(solution)/shard_map/ppermute | solution.py:22
  288.7 22.2 %copy-start.1 = (f32[3,4096]{0,1:T(8,128)S(1)}, f32[3,4096]{0,1:T(8,128)}, u32[]{:S(2)}) copy-start(f32[3,4096]{0,1:T(8,128)} %get-tuple-element.718) | copy-start | bytes 147460
  288.8 7.1 %collective-permute-start.15 = (f32[3,9,2,256]{3,1,2,0:T(8,128)S(1)}, f32[3,9,2,256]{3,1,2,0:T(8,128)S(1)}, u32[]{:S(2)}, u32[]{:S(2)}) collective-permute-start(f32[3,9,2,256]{3,1,2,0:T(8,128)S(1)} %copy.359), channel_id=1, source_target_pairs={{0,8},{8,16},{16,24},{24,32},{32,40},{40,48},{48,56},{56,64},{64,7... | collective-permute-start | bytes 165896 | tf_op jit(solution)/shard_map/ppermute | solution.py:22
  293.0 13.2 %collective-permute-start.14 = (f32[3,9,2,256]{3,1,2,0:T(8,128)S(1)}, f32[3,9,2,256]{3,1,2,0:T(8,128)S(1)}, u32[]{:S(2)}, u32[]{:S(2)}) collective-permute-start(f32[3,9,2,256]{3,1,2,0:T(8,128)S(1)} %copy.358), channel_id=1, source_target_pairs={{8,0},{16,8},{24,16},{32,24},{40,32},{48,40},{56,48},{64,56},{72,6... | collective-permute-start | bytes 165896 | tf_op jit(solution)/shard_map/ppermute | solution.py:23
  307.4 18.1 %all-to-all-start.3 = ((f32[8,2,9,3,256]{4,1,3,2,0:T(2,128)}), f32[8,2,9,3,256]{4,1,3,2,0:T(2,128)S(1)}, u32[]{:S(2)}, u32[]{:S(2)}) async-start(f32[8,2,9,3,256]{4,1,3,2,0:T(2,128)} %stack.143), calls=%async_computation.3 | async-start | bytes 884736 | tf_op jit(solution)/shard_map/all_to_all | solution.py:151
